TPU v7x, 128 devices: a whole 4x4x4 slice. The times are simulated.
128 devices in a mesh: dp: 16 (over y, x_hi, core), tensor: 8 (over z, x_lo).
Axes of the slice: x: 4 (x_hi: 2, x_lo: 2; x = x_hi * 2 + x_lo), y: 4, z: 4, core: 2. Of those that a mesh axis runs over, the one named last changes fastest.
Arguments:
- tokens: bfloat16 [8192, 4096], P(('dp', 'tensor')), may hold values from -24 to 24
- w_up: bfloat16 [4096, 8192], P(None, 'tensor'), may hold values from -0.125 to 0.125
- w_down: bfloat16 [8192, 4096], P('tensor'), may hold values from -0.09375 to 0.09375
- mask_up: int32 [64, 128], P(None, 'tensor'), may hold values from 0 to 1, as said below
- mask_down: int32 [128, 64], P('tensor'), may hold values from 0 to 1, as said below
- cotangent: bfloat16 [8192, 4096], P(('dp', 'tensor')), may hold values from -24 to 24
Outputs:
- output: bfloat16 [8192, 4096], P(('dp', 'tensor'))
- grad_tokens: bfloat16 [8192, 4096], P(('dp', 'tensor'))
- grad_up: float32 [4096, 8192], P('dp', 'tensor')
- grad_down: float32 [8192, 4096], P('tensor', 'dp')
Inputs may be any that keep to these rules, and one draw needn't show every extreme that they name: `mask_up`: split into aligned groups of 4 block rows by 16 block columns, every group keeps at most 40 blocks, and some group keeps exactly 40. `mask_down`: split into aligned groups of 16 block rows by 4 block columns, every group keeps at most 40 blocks, and some group keeps exactly 40.
All inputs are finite; a program needn't handle non-finite values.
Results may differ from a plain program's by a relative error of at most 0.019.
Values may be sent and summed in bfloat16 or wider, within the bound.
No kernel may reach another device: no remote copies, remote signals or barrier semaphores. Data moves between devices by JAX's collectives and lax.ppermute only.
A program may use at most 256 MiB of HBM per device.

v0:
```python
import math
import jax
import jax.numpy as jnp
from jax import lax
from jax.sharding import PartitionSpec as P

B = 64


def gelu_tanh(value):
    inner = math.sqrt(2.0 / math.pi) * (value + 0.044715 * value * value * value)
    return 0.5 * value * (1.0 + jnp.tanh(inner))


def gelu_slope(value):
    coeff = math.sqrt(2.0 / math.pi)
    tanh_part = jnp.tanh(coeff * (value + 0.044715 * value * value * value))
    return 0.5 * (1.0 + tanh_part) + 0.5 * value * (1.0 - tanh_part * tanh_part) * coeff * (
        1.0 + 3.0 * 0.044715 * value * value
    )


def apply_mask(weight, mask):
    nrows, ncols = mask.shape
    shaped = weight.reshape(nrows, B, ncols, B) * mask.astype(weight.dtype)[:, None, :, None]
    return shaped.reshape(weight.shape)


def local(tokens, w_up, w_down, mask_up, mask_down, cotangent):
    rows_x, rows_dy = (
        lax.all_gather(tokens, "tensor", axis=0, tiled=True),
        lax.all_gather(cotangent, "tensor", axis=0, tiled=True),
    )
    up_kept = apply_mask(w_up, mask_up)
    down_kept = apply_mask(w_down, mask_down)
    pre = jnp.dot(rows_x, up_kept, preferred_element_type=jnp.float32)
    hidden = gelu_tanh(pre).astype(jnp.bfloat16)
    piece = hidden
    output = lax.psum_scatter(
        jnp.dot(piece, down_kept, preferred_element_type=jnp.float32).astype(jnp.bfloat16),
        "tensor",
        scatter_dimension=0,
        tiled=True,
    )
    local_down = lax.dot_general(
        hidden, rows_dy, (((0,), (0,)), ((), ())), preferred_element_type=jnp.float32
    )
    local_down = apply_mask(local_down, mask_down)
    grad_down = lax.psum_scatter(
        local_down.astype(jnp.bfloat16), "dp", scatter_dimension=1, tiled=True
    ).astype(jnp.float32)
    grad_hidden = lax.dot_general(
        rows_dy, down_kept, (((1,), (1,)), ((), ())), preferred_element_type=jnp.float32
    )
    grad_pre = (grad_hidden * gelu_slope(pre)).astype(jnp.bfloat16)
    piece = grad_pre
    grad_tokens = lax.psum_scatter(
        lax.dot_general(
            piece, up_kept, (((1,), (1,)), ((), ())), preferred_element_type=jnp.float32
        ).astype(jnp.bfloat16),
        "tensor",
        scatter_dimension=0,
        tiled=True,
    )
    local_up = lax.dot_general(
        rows_x, grad_pre, (((0,), (0,)), ((), ())), preferred_element_type=jnp.float32
    )
    local_up = apply_mask(local_up, mask_up)
    grad_up = lax.psum_scatter(
        local_up.astype(jnp.bfloat16), "dp", scatter_dimension=0, tiled=True
    ).astype(jnp.float32)
    return (output, grad_tokens, grad_up, grad_down)


def solution(mesh):
    placed = (
        P(("dp", "tensor"), None),
        P(None, "tensor"),
        P("tensor", None),
        P(None, "tensor"),
        P("tensor", None),
        P(("dp", "tensor"), None),
    )
    return jax.shard_map(
        local,
        mesh=mesh,
        in_specs=placed,
        out_specs=(
            P(("dp", "tensor"), None),
            P(("dp", "tensor"), None),
            P("dp", "tensor"),
            P("tensor", "dp"),
        ),
        check_vma=False,
    )
```

profile of v0, /device:TPU:1, one launch (start us, length us, event | category | flops | bytes accessed | tf_op | source)
XLA Modules:
  0.0 609.4 jit_solution(7236030214603168126)
XLA Ops:
  7.2 0.0 all-gather.3.cloned.1.call-start
  7.2 0.7 all-gather.3.cloned.1.call-update
  7.9 0.0 all-gather.5.cloned.1.call-start
  7.9 0.7 all-gather.5.cloned.1.call-update
  8.6 0.0 reduce-scatter.11.cloned.1.call-start
  8.7 0.8 fusion.17
  9.5 0.1 copy.10
  9.6 6.1 %mul.94 = bf16[64,64,16,64]{3,2,1,0:T(8,128)(2,1)} broadcast(bf16[64,16]{1,0:T(8,128)(2,1)S(1)} %copy.10), dimensions={0,2} | broadcast | bytes 8390656 | tf_op jit(solution)/shard_map/mul | solution.py:25
  15.7 22.6 %mul.95 = bf16[4096,1024]{1,0:T(8,128)(2,1)} reshape(bf16[64,64,16,64]{3,2,1,0:T(8,128)(2,1)} %mul.94) | data formatting | bytes 16777216 | tf_op jit(solution)/shard_map/mul | solution.py:25
  38.3 11.4 %mul.118 = f32[16,64,64,64]{3,2,1,0:T(8,128)} broadcast(f32[16,64]{1,0:T(8,128)S(1)} %get-tuple-element.8), dimensions={0,2} | broadcast | bytes 16781312 | tf_op jit(solution)/shard_map/mul | solution.py:25
  49.7 28.0 %mul.119 = f32[1024,4096]{1,0:T(8,128)} reshape(f32[16,64,64,64]{3,2,1,0:T(8,128)} %mul.118) | data formatting | bytes 33554432 | tf_op jit(solution)/shard_map/mul | solution.py:25
  77.7 25.9 %all-gather.3.cloned.1.call-done = bf16[512,4096]{1,0:T(8,128)(2,1)} async-done(((bf16[64,4096]{1,0:T(8,128)(2,1)}), bf16[512,4096]{1,0:T(8,128)(2,1)}) %all-gather.3.cloned.1.call-update) | async-done | bytes 4194320 | tf_op jit(solution)/shard_map/all_gather | solution.py:31
  103.6 9.5 %fusion.5 = f32[1024,512]{1,0:T(8,128)S(1)} fusion(bf16[512,4096]{1,0:T(8,128)(2,1)} %all-gather.3.cloned.1.call-done, bf16[4096,1024]{1,0:T(8,128)(2,1)} %param.7, bf16[4096,1024]{1,0:T(8,128)(2,1)} %mul.95), kind=kOutput, calls=%fused_computation.9 | convolution fusion | flops 4299161600 | bytes 23068672 | tf_op jit(solution)/shard_map/dot_general | solution.py:36
  113.1 82.9 %all-gather.5.cloned.1.call-done = bf16[512,4096]{1,0:T(8,128)(2,1)} async-done(((bf16[64,4096]{1,0:T(8,128)(2,1)}), bf16[512,4096]{1,0:T(8,128)(2,1)}) %all-gather.5.cloned.1.call-update) | async-done | bytes 4194320 | tf_op jit(solution)/shard_map/all_gather | solution.py:32
  196.1 11.4 %multiply_convert_fusion = bf16[1024,4096]{1,0:T(8,128)(2,1)} fusion(f32[1024,4096]{1,0:T(8,128)} %mul.119, bf16[512,4096]{1,0:T(8,128)(2,1)} %all-gather.5.cloned.1.call-done, f32[1024,512]{1,0:T(8,128)S(1)} %fusion.5), kind=kOutput, calls=%fused_computation.2 | convolution fusion | flops 4308074496 | bytes 31457280 | tf_op jit(solution)/shard_map/dot_general | solution.py:45
  207.5 0.2 reduce-scatter.9.cloned.1.call-start
  207.8 6.5 %mul.103 = bf16[16,64,64,64]{3,2,1,0:T(8,128)(2,1)} broadcast(bf16[16,64]{1,0:T(8,128)(2,1)S(1)} %get-tuple-element.9), dimensions={0,2} | broadcast | bytes 8390656 | tf_op jit(solution)/shard_map/mul | solution.py:25
  214.2 23.2 %mul.104 = bf16[1024,4096]{1,0:T(8,128)(2,1)} reshape(bf16[16,64,64,64]{3,2,1,0:T(8,128)(2,1)} %mul.103) | data formatting | bytes 16777216 | tf_op jit(solution)/shard_map/mul | solution.py:25
  237.4 11.6 %mul.115 = f32[64,64,16,64]{1,0,3,2:T(8,128)} broadcast(f32[64,16]{0,1:T(8,128)S(1)} %get-tuple-element.10), dimensions={0,2} | broadcast | bytes 16781312 | tf_op jit(solution)/shard_map/mul | solution.py:25
  249.0 28.2 %mul.116 = f32[4096,1024]{0,1:T(8,128)} reshape(f32[64,64,16,64]{1,0,3,2:T(8,128)} %mul.115) | data formatting | bytes 33554432 | tf_op jit(solution)/shard_map/mul | solution.py:25
  277.2 12.8 %fusion.13 = bf16[512,1024]{0,1:T(8,128)(2,1)S(1)} fusion(f32[1024,512]{1,0:T(8,128)S(1)} %fusion.5, bf16[512,4096]{1,0:T(8,128)(2,1)} %all-gather.5.cloned.1.call-done, bf16[1024,4096]{1,0:T(8,128)(2,1)} %param.8, bf16[1024,4096]{1,0:T(8,128)(2,1)} %mul.104), kind=kOutput, calls=%fused_computation.19 | convolution fusion | flops 4309123072 | bytes 24117248 | tf_op jit(solution)/shard_map/dot_general | solution.py:52
  290.0 10.6 %fusion = bf16[4096,1024]{0,1:T(8,128)(2,1)} fusion(f32[4096,1024]{0,1:T(8,128)} %mul.116, bf16[512,1024]{0,1:T(8,128)(2,1)S(1)} %fusion.13, bf16[512,4096]{1,0:T(8,128)(2,1)S(1)} %copy-done), kind=kOutput, calls=%fused_computation.1 | convolution fusion | flops 4303355904 | bytes 30408704 | tf_op jit(solution)/shard_map/dot_general | solution.py:65
  300.6 0.0 reduce-scatter.7.cloned.1.call-start
  300.7 12.8 %convolution_convert_fusion = bf16[512,4096]{1,0:T(8,128)(2,1)} fusion(bf16[512,1024]{0,1:T(8,128)(2,1)S(1)} %fusion.13, bf16[4096,1024]{1,0:T(8,128)(2,1)} %param.7, bf16[4096,1024]{1,0:T(8,128)(2,1)} %mul.95), kind=kOutput, calls=%fused_computation.3 | convolution fusion | flops 4301258752 | bytes 22020096 | tf_op jit(solution)/shard_map/dot_general | solution.py:58
  313.5 0.3 reduce-scatter.5.cloned.1.call-start
  313.8 12.4 %convolution_convert_fusion.1 = bf16[512,4096]{1,0:T(8,128)(2,1)} fusion(bf16[1024,4096]{1,0:T(8,128)(2,1)} %param.8, bf16[1024,4096]{1,0:T(8,128)(2,1)} %mul.104, f32[1024,512]{1,0:T(8,128)S(1)} %fusion.5), kind=kOutput, calls=%fused_computation.4 | convolution fusion | flops 4305977344 | bytes 23068672 | tf_op jit(solution)/shard_map/dot_general | solution.py:40
  326.3 0.0 reduce-scatter.11.cloned.1.call-done
  326.3 2.2 convert_element_type.47
  328.5 85.9 %reduce-scatter.9.cloned.1.call-done = bf16[256,1024]{0,1:T(8,128)(2,1)} async-done(((bf16[4096,1024]{0,1:T(8,128)(2,1)}), bf16[256,1024]{0,1:T(8,128)(2,1)}) %reduce-scatter.9.cloned.1.call-update) | async-done | bytes 524304 | tf_op jit(solution)/shard_map/reduce_scatter | solution.py:69
  414.4 2.2 copy.11
  416.6 91.8 %reduce-scatter.7.cloned.1.call-done = bf16[64,4096]{1,0:T(8,128)(2,1)} async-done(((bf16[512,4096]{1,0:T(8,128)(2,1)}), bf16[64,4096]{1,0:T(8,128)(2,1)}) %reduce-scatter.7.cloned.1.call-update) | async-done | bytes 524304 | tf_op jit(solution)/shard_map/reduce_scatter | solution.py:57
  508.4 94.1 %reduce-scatter.5.cloned.1.call-done = bf16[64,4096]{1,0:T(8,128)(2,1)} async-done(((bf16[512,4096]{1,0:T(8,128)(2,1)}), bf16[64,4096]{1,0:T(8,128)(2,1)}) %reduce-scatter.5.cloned.1.call-update) | async-done | bytes 524304 | tf_op jit(solution)/shard_map/reduce_scatter | solution.py:39
  (9 shorter events, 0.1 us)
Async XLA Ops:
  7.2 96.5 %all-gather.3.cloned.1.call-start = ((), (), s32[]{:S(2)}) async-start(), calls=%async_computation.4 | async-start | bytes 4718592 | tf_op jit(solution)/shard_map/all_gather | solution.py:31
  7.9 188.2 %all-gather.5.cloned.1.call-start = ((), (), s32[]{:S(2)}) async-start(), calls=%async_computation.6 | async-start | bytes 4718592 | tf_op jit(solution)/shard_map/all_gather | solution.py:32
  8.6 317.7 %reduce-scatter.11.cloned.1.call-start = ((), (), s32[]{:S(2)}) async-start(), calls=%async_computation.9 | async-start | bytes 8912896 | tf_op jit(solution)/shard_map/reduce_scatter | solution.py:49
  15.7 22.6 %copy-start.1 = (s32[16,64]{1,0:T(8,128)S(1)}, s32[16,64]{1,0:T(8,128)}, u32[]{:S(2)}) copy-start(s32[16,64]{1,0:T(8,128)} %param.10) | copy-start | bytes 12292
  207.5 206.9 %reduce-scatter.9.cloned.1.call-start = ((), (), s32[]{:S(2)}) async-start(), calls=%async_computation.8 | async-start | bytes 8912896 | tf_op jit(solution)/shard_map/reduce_scatter | solution.py:69
  277.2 12.8 %copy-start = (bf16[512,4096]{1,0:T(8,128)(2,1)S(1)}, bf16[512,4096]{1,0:T(8,128)(2,1)}, u32[]{:S(2)}) copy-start(bf16[512,4096]{1,0:T(8,128)(2,1)} %all-gather.3.cloned.1.call-done) | copy-start | bytes 12582916
  300.6 207.8 %reduce-scatter.7.cloned.1.call-start = ((), (), s32[]{:S(2)}) async-start(), calls=%async_computation.7 | async-start | bytes 4718592 | tf_op jit(solution)/shard_map/reduce_scatter | solution.py:57
  313.5 289.0 %reduce-scatter.5.cloned.1.call-start = ((), (), s32[]{:S(2)}) async-start(), calls=%async_computation.5 | async-start | bytes 4718592 | tf_op jit(solution)/shard_map/reduce_scatter | solution.py:39
Sparse Core Ops, SparseCore 0:
  9.6 93.9 all-gather.2
  105.3 90.7 all-gather.4
  207.6 101.3 reduce-scatter.10
  313.2 101.1 reduce-scatter.8
  417.3 91.1 reduce-scatter.6
  511.2 91.2 reduce-scatter.4
where the time goes:
time: 611 us; the launch traced here: 609 us
  waiting for transfers between devices  382 us (63%)
  local copies, waits for them, and re-layouts  140 us (23%)
  matrix products  69.6 us (11%)
  between operations  14.1 us (2%)
    mul x8, local copies, waits for them, and re-layouts, apply_mask(): weight.reshape(nrows, B, ncols, B)  138 us
    reduce_scatter x1, waiting for transfers between devices, local(): lax.psum_scatter(jnp.dot(piece, down_kept, preferred_element_type=jnp.flo...  94.1 us
    reduce_scatter x1, waiting for transfers between devices, local(): lax.psum_scatter(lax.dot_general(piece, up_kept, (((1,), (1,)), ((), ()))...  91.8 us
    reduce_scatter x1, waiting for transfers between devices, local(): lax.psum_scatter(local_up.astype(jnp.bfloat16), 'dp', scatter_dimension=0...  85.9 us
    all_gather x1, waiting for transfers between devices, local(): lax.all_gather(cotangent, 'tensor', axis=0, tiled=True)  82.9 us
    all_gather x1, waiting for transfers between devices, local(): lax.all_gather(tokens, 'tensor', axis=0, tiled=True)  25.9 us
    dot_general x1, matrix products, local(): lax.dot_general(piece, up_kept, (((1,), (1,)), ((), ())), preferred_eleme...  12.8 us
    dot_general x1, matrix products, local(): lax.dot_general(rows_dy, down_kept, (((1,), (1,)), ((), ())), preferred_e...  12.8 us
  transfers between devices with their start and end apart: 6, of which 5 were waited for; matrix products, arithmetic and copies ran while one was open for 33% of the time, Pallas kernels for 0%

commit v1 on v0

--- a/solution.py
+++ b/solution.py
@@ -28,7 +28,9 @@
 
 def local(tokens, w_up, w_down, mask_up, mask_down, cotangent):
     rows_x, rows_dy = (
-        lax.all_gather(tokens, "tensor", axis=0, tiled=True),
+        jnp.concatenate(
+            lax.all_to_all(jnp.stack([tokens] * lax.axis_size("tensor")), "tensor", 0, 0), axis=0
+        ),
         lax.all_gather(cotangent, "tensor", axis=0, tiled=True),
     )
     up_kept = apply_mask(w_up, mask_up)

time: 611 us -> 561 us (0.918)
  waiting for transfers between devices: 382 us -> 322 us
  starting transfers between devices: 0.64 us -> 7.52 us
    all_gather x1, waiting for transfers between devices: 82.9 us -> 28.9 us  [local(): lax.all_gather(cotangent, 'tensor', axis=0, tiled=True)]
    all_gather x1 -> x0, waiting for transfers between devices: 25.9 us -> none  [local(): lax.all_gather(tokens, 'tensor', axis=0, tiled=True)]
    all_to_all x0 -> x1, waiting for transfers between devices: none -> 21.2 us  [local(): lax.all_to_all(jnp.stack([tokens] * lax.axis_size('tensor')), 'tensor', 0...]
    all_to_all x0 -> x1, starting transfers between devices: none -> 6.92 us  [local(): lax.all_to_all(jnp.stack([tokens] * lax.axis_size('tensor')), 'tensor', 0...]
  transfers between devices with their start and end apart: 6 -> 6, of which waited for: 5 -> 5; matrix products, arithmetic and copies ran while one was open for 33% -> 37% of each run, Pallas kernels for 0% -> 0%
where the time goes in v1:
time: 561 us; the launch traced here: 559 us
  waiting for transfers between devices  322 us (57%)
  local copies, waits for them, and re-layouts  143 us (25%)
  matrix products  70.6 us (13%)
  between operations  13.8 us (2%)
  starting transfers between devices  7.52 us (1%)
    mul x8, local copies, waits for them, and re-layouts, apply_mask(): weight.reshape(nrows, B, ncols, B)  137 us
    reduce_scatter x1, waiting for transfers between devices, local(): lax.psum_scatter(lax.dot_general(piece, up_kept, (((1,), (1,)), ((), ()))...  94.1 us
    reduce_scatter x1, waiting for transfers between devices, local(): lax.psum_scatter(jnp.dot(piece, down_kept, preferred_element_type=jnp.flo...  91.8 us
    reduce_scatter x1, waiting for transfers between devices, local(): lax.psum_scatter(local_up.astype(jnp.bfloat16), 'dp', scatter_dimension=0...  85.1 us
    all_gather x1, waiting for transfers between devices, local(): lax.all_gather(cotangent, 'tensor', axis=0, tiled=True)  28.9 us
    all_to_all x1, waiting for transfers between devices, local(): lax.all_to_all(jnp.stack([tokens] * lax.axis_size('tensor')), 'tensor', 0...  21.2 us
    dot_general x1, matrix products, local(): jnp.dot(piece, down_kept, preferred_element_type=jnp.float32)  12.7 us
    dot_general x1, matrix products, local(): lax.dot_general(rows_dy, down_kept, (((1,), (1,)), ((), ())), preferred_e...  12.6 us
  transfers between devices with their start and end apart: 6, of which 5 were waited for; matrix products, arithmetic and copies ran while one was open for 37% of the time, Pallas kernels for 0%

profile of v1, /device:TPU:1, one launch (start us, length us, event | category | flops | bytes accessed | tf_op | source)
XLA Modules:
  0.0 559.2 jit_solution(1591828521832208834)
XLA Ops:
  7.2 0.0 all-gather.2.cloned.1.call-start
  7.2 0.7 all-gather.2.cloned.1.call-update
  7.9 3.5 stack.2
  11.4 6.9 %all-to-all-start = ((bf16[8,64,4096]{2,1,0:T(8,128)(2,1)}), bf16[8,64,4096]{2,1,0:T(8,128)(2,1)}, u32[]{:S(2)}, u32[]{:S(2)}) async-start(bf16[8,64,4096]{2,1,0:T(8,128)(2,1)} %stack.2), calls=%async_computation | async-start | bytes 8388608 | tf_op jit(solution)/shard_map/all_to_all | solution.py:32
  18.3 0.0 reduce-scatter.11.cloned.1.call-start
  18.4 0.1 copy.10
  18.5 6.1 %mul.94 = bf16[64,64,16,64]{3,2,1,0:T(8,128)(2,1)} broadcast(bf16[64,16]{1,0:T(8,128)(2,1)S(1)} %copy.10), dimensions={0,2} | broadcast | bytes 8390656 | tf_op jit(solution)/shard_map/mul | solution.py:25
  24.6 22.6 %mul.95 = bf16[4096,1024]{1,0:T(8,128)(2,1)} reshape(bf16[64,64,16,64]{3,2,1,0:T(8,128)(2,1)} %mul.94) | data formatting | bytes 16777216 | tf_op jit(solution)/shard_map/mul | solution.py:25
  47.2 11.4 %mul.118 = f32[16,64,64,64]{3,2,1,0:T(8,128)} broadcast(f32[16,64]{1,0:T(8,128)S(1)} %get-tuple-element.8), dimensions={0,2} | broadcast | bytes 16781312 | tf_op jit(solution)/shard_map/mul | solution.py:25
  58.6 28.0 %mul.119 = f32[1024,4096]{1,0:T(8,128)} reshape(f32[16,64,64,64]{3,2,1,0:T(8,128)} %mul.118) | data formatting | bytes 33554432 | tf_op jit(solution)/shard_map/mul | solution.py:25
  86.6 21.2 %all-to-all-done = bf16[8,64,4096]{2,1,0:T(8,128)(2,1)} async-done(((bf16[8,64,4096]{2,1,0:T(8,128)(2,1)}), bf16[8,64,4096]{2,1,0:T(8,128)(2,1)}, u32[]{:S(2)}, u32[]{:S(2)}) %all-to-all-start) | async-done | bytes 4194336 | tf_op jit(solution)/shard_map/all_to_all | solution.py:32
  107.7 9.5 %fusion.5 = f32[1024,512]{1,0:T(8,128)S(1)} fusion(bf16[512,4096]{1,0:T(8,128)(2,1)} %bitcast, bf16[4096,1024]{1,0:T(8,128)(2,1)} %param.7, bf16[4096,1024]{1,0:T(8,128)(2,1)} %mul.95), kind=kOutput, calls=%fused_computation.9 | convolution fusion | flops 4299161600 | bytes 23068672 | tf_op jit(solution)/shard_map/dot_general | solution.py:38
  117.3 28.9 %all-gather.2.cloned.1.call-done = bf16[512,4096]{1,0:T(8,128)(2,1)} async-done(((bf16[64,4096]{1,0:T(8,128)(2,1)}), bf16[512,4096]{1,0:T(8,128)(2,1)}) %all-gather.2.cloned.1.call-update) | async-done | bytes 4194320 | tf_op jit(solution)/shard_map/all_gather | solution.py:34
  146.1 11.5 %multiply_convert_fusion = bf16[1024,4096]{1,0:T(8,128)(2,1)} fusion(f32[1024,4096]{1,0:T(8,128)} %mul.119, bf16[512,4096]{1,0:T(8,128)(2,1)} %all-gather.2.cloned.1.call-done, f32[1024,512]{1,0:T(8,128)S(1)} %fusion.5), kind=kOutput, calls=%fused_computation.2 | convolution fusion | flops 4308074496 | bytes 31457280 | tf_op jit(solution)/shard_map/dot_general | solution.py:47
  157.6 0.0 reduce-scatter.11.cloned.1.call-update
  157.6 0.2 reduce-scatter.9.cloned.1.call-start
  157.8 6.5 %mul.103 = bf16[16,64,64,64]{3,2,1,0:T(8,128)(2,1)} broadcast(bf16[16,64]{1,0:T(8,128)(2,1)S(1)} %get-tuple-element.9), dimensions={0,2} | broadcast | bytes 8390656 | tf_op jit(solution)/shard_map/mul | solution.py:25
  164.3 23.2 %mul.104 = bf16[1024,4096]{1,0:T(8,128)(2,1)} reshape(bf16[16,64,64,64]{3,2,1,0:T(8,128)(2,1)} %mul.103) | data formatting | bytes 16777216 | tf_op jit(solution)/shard_map/mul | solution.py:25
  187.5 11.6 %mul.115 = f32[64,64,16,64]{1,0,3,2:T(8,128)} broadcast(f32[64,16]{0,1:T(8,128)S(1)} %get-tuple-element.10), dimensions={0,2} | broadcast | bytes 16781312 | tf_op jit(solution)/shard_map/mul | solution.py:25
  199.1 28.2 %mul.116 = f32[4096,1024]{0,1:T(8,128)} reshape(f32[64,64,16,64]{1,0,3,2:T(8,128)} %mul.115) | data formatting | bytes 33554432 | tf_op jit(solution)/shard_map/mul | solution.py:25
  227.2 12.6 %fusion.13 = bf16[512,1024]{0,1:T(8,128)(2,1)S(1)} fusion(f32[1024,512]{1,0:T(8,128)S(1)} %fusion.5, bf16[512,4096]{1,0:T(8,128)(2,1)} %all-gather.2.cloned.1.call-done, bf16[1024,4096]{1,0:T(8,128)(2,1)} %param.8, bf16[1024,4096]{1,0:T(8,128)(2,1)} %mul.104), kind=kOutput, calls=%fused_computation.19 | convolution fusion | flops 4309123072 | bytes 24117248 | tf_op jit(solution)/shard_map/dot_general | solution.py:54
  239.9 11.7 %fusion = bf16[4096,1024]{0,1:T(8,128)(2,1)} fusion(f32[4096,1024]{0,1:T(8,128)} %mul.116, bf16[512,1024]{0,1:T(8,128)(2,1)S(1)} %fusion.13, bf16[512,4096]{1,0:T(8,128)(2,1)} %bitcast), kind=kOutput, calls=%fused_computation.1 | convolution fusion | flops 4303355904 | bytes 30408704 | tf_op jit(solution)/shard_map/dot_general | solution.py:67
  251.6 0.0 reduce-scatter.5.cloned.1.call-start
  251.7 12.7 %convolution_convert_fusion.1 = bf16[512,4096]{1,0:T(8,128)(2,1)} fusion(bf16[1024,4096]{1,0:T(8,128)(2,1)} %param.8, bf16[1024,4096]{1,0:T(8,128)(2,1)} %mul.104, f32[1024,512]{1,0:T(8,128)S(1)} %fusion.5), kind=kOutput, calls=%fused_computation.4 | convolution fusion | flops 4305977344 | bytes 23068672 | tf_op jit(solution)/shard_map/dot_general | solution.py:42
  264.4 0.3 reduce-scatter.7.cloned.1.call-start
  264.7 12.6 %convolution_convert_fusion = bf16[512,4096]{1,0:T(8,128)(2,1)} fusion(bf16[512,1024]{0,1:T(8,128)(2,1)S(1)} %fusion.13, bf16[4096,1024]{1,0:T(8,128)(2,1)} %param.7, bf16[4096,1024]{1,0:T(8,128)(2,1)} %mul.95), kind=kOutput, calls=%fused_computation.3 | convolution fusion | flops 4301258752 | bytes 22020096 | tf_op jit(solution)/shard_map/dot_general | solution.py:60
  277.2 0.0 reduce-scatter.11.cloned.1.call-done
  277.3 2.1 convert_element_type.47
  279.4 85.1 %reduce-scatter.9.cloned.1.call-done = bf16[256,1024]{0,1:T(8,128)(2,1)} async-done(((bf16[4096,1024]{0,1:T(8,128)(2,1)}), bf16[256,1024]{0,1:T(8,128)(2,1)}) %reduce-scatter.9.cloned.1.call-update) | async-done | bytes 524304 | tf_op jit(solution)/shard_map/reduce_scatter | solution.py:71
  364.5 2.2 copy.11
  366.7 91.8 %reduce-scatter.5.cloned.1.call-done = bf16[64,4096]{1,0:T(8,128)(2,1)} async-done(((bf16[512,4096]{1,0:T(8,128)(2,1)}), bf16[64,4096]{1,0:T(8,128)(2,1)}) %reduce-scatter.5.cloned.1.call-update) | async-done | bytes 524304 | tf_op jit(solution)/shard_map/reduce_scatter | solution.py:41
  458.5 94.1 %reduce-scatter.7.cloned.1.call-done = bf16[64,4096]{1,0:T(8,128)(2,1)} async-done(((bf16[512,4096]{1,0:T(8,128)(2,1)}), bf16[64,4096]{1,0:T(8,128)(2,1)}) %reduce-scatter.7.cloned.1.call-update) | async-done | bytes 524304 | tf_op jit(solution)/shard_map/reduce_scatter | solution.py:59
  (9 shorter events, 0.1 us)
Async XLA Ops:
  7.2 139.0 %all-gather.2.cloned.1.call-start = ((), (), s32[]{:S(2)}) async-start(), calls=%async_computation.6 | async-start | bytes 4718592 | tf_op jit(solution)/shard_map/all_gather | solution.py:34
  11.4 7.0 %copy-start = (s32[64,16]{0,1:T(8,128)S(1)}, s32[64,16]{0,1:T(8,128)}, u32[]{:S(2)}) copy-start(s32[64,16]{0,1:T(8,128)} %param.9) | copy-start | bytes 12292
  11.4 96.3 %all-to-all-start = ((bf16[8,64,4096]{2,1,0:T(8,128)(2,1)}), bf16[8,64,4096]{2,1,0:T(8,128)(2,1)}, u32[]{:S(2)}, u32[]{:S(2)}) async-start(bf16[8,64,4096]{2,1,0:T(8,128)(2,1)} %stack.2), calls=%async_computation | async-start | bytes 8388608 | tf_op jit(solution)/shard_map/all_to_all | solution.py:32
  18.3 258.9 %reduce-scatter.11.cloned.1.call-start = ((), (), s32[]{:S(2)}) async-start(), calls=%async_computation.9 | async-start | bytes 8912896 | tf_op jit(solution)/shard_map/reduce_scatter | solution.py:51
  24.6 22.6 %copy-start.1 = (s32[16,64]{1,0:T(8,128)S(1)}, s32[16,64]{1,0:T(8,128)}, u32[]{:S(2)}) copy-start(s32[16,64]{1,0:T(8,128)} %param.10) | copy-start | bytes 12292
  157.6 206.9 %reduce-scatter.9.cloned.1.call-start = ((), (), s32[]{:S(2)}) async-start(), calls=%async_computation.8 | async-start | bytes 8912896 | tf_op jit(solution)/shard_map/reduce_scatter | solution.py:71
  251.6 206.9 %reduce-scatter.5.cloned.1.call-start = ((), (), s32[]{:S(2)}) async-start(), calls=%async_computation.5 | async-start | bytes 4718592 | tf_op jit(solution)/shard_map/reduce_scatter | solution.py:41
  264.4 288.3 %reduce-scatter.7.cloned.1.call-start = ((), (), s32[]{:S(2)}) async-start(), calls=%async_computation.7 | async-start | bytes 4718592 | tf_op jit(solution)/shard_map/reduce_scatter | solution.py:59
Sparse Core Ops, SparseCore 0:
  9.6 136.4 all-gather.1
  157.7 101.3 reduce-scatter.10
  263.4 101.0 reduce-scatter.8
  367.3 91.1 reduce-scatter.4
  461.3 91.2 reduce-scatter.6
